TPU v7x, 32 devices: a whole 2x2x4 slice. The times are simulated.
32 devices in a mesh: row: 4 (over y, x), col: 8 (over z, core).
Axes of the slice: x: 2, y: 2, z: 4, core: 2. Of those that a mesh axis runs over, the one named last changes fastest.
Arguments:
- factor: bfloat16 [4, 12, 512, 8, 1, 512], P('row', None, None, 'col'), may hold values from -0.03125 to 0.03125, as said below
- diag_inverse: float32 [4, 2, 1024, 512], P('row'), may hold values from -0.088388348 to 1.5, as said below
- residuals: float32 [256, 12, 4, 512], P('row', None, None, 'col'), may hold values from -6 to 6
Outputs:
- solved: float32 [256, 2, 4, 512], P('col', None, 'row')
- trailing: float32 [256, 10, 4, 512], P('col', None, 'row')
Inputs may be any that keep to these rules, and one draw needn't show every extreme that they name: factor is zero wherever its row block halved (rounded down) is not above its column block halved. `diag_inverse`: each pair's inverse, assembled from its two blocks' columns, is lower triangular with diagonal entries from 0.5 to 1.5.
All inputs are finite; a program needn't handle non-finite values.
Results may differ from a plain program's by a relative error of at most 0.0095.
Values may be sent and summed in bfloat16 or wider, within the bound.
A program may use at most 64 MiB of HBM per device.

v0:
```python
import jax
import jax.numpy as jnp
from jax import lax
from jax.sharding import PartitionSpec as P


def shards(factor, diag_inverse, residuals):
    row_count = lax.axis_size("row")
    col_count = lax.axis_size("col")
    my_row = lax.axis_index("row")
    my_col = lax.axis_index("col")
    local_factor = factor[0, :, :, 0]
    blocks_here = local_factor.shape[0]
    block_width = local_factor.shape[1]
    panel_count = local_factor.shape[2]
    flat_factor = local_factor.reshape(blocks_here, block_width, panel_count * block_width)
    inverses = diag_inverse[0]
    diag_blocks = inverses.shape[0]
    relaid = lax.all_to_all(
        lax.all_to_all(
            residuals.astype(jnp.bfloat16), "row", split_axis=2, concat_axis=0, tiled=True
        ),
        "col",
        split_axis=0,
        concat_axis=3,
        tiled=True,
    ).astype(residuals.dtype)
    own_rhs = relaid[:, :, 0, :]
    slice_width = own_rhs.shape[0]
    walker_total = slice_width * col_count
    pair_total = panel_count * col_count // 2
    known_start = jnp.zeros((walker_total, panel_count * block_width), jnp.bfloat16)
    solved_start = jnp.zeros((slice_width, diag_blocks, block_width), jnp.float32)
    walker_start = my_col * slice_width

    def one_pair(pair_index, loop_state):
        known_blocks, solved_local = loop_state
        first_block = (2 * jnp.asarray(pair_index)).astype(jnp.int32)
        local_block = first_block // row_count
        first_row = first_block % row_count
        is_second = my_row == first_row + 1
        owns = jnp.logical_or(my_row == first_row, is_second)
        block_factor = lax.dynamic_index_in_dim(flat_factor, local_block, 0, keepdims=False)
        partial_value = lax.dot_general(
            known_blocks, block_factor, (((1,), (1,)), ((), ())), preferred_element_type=jnp.float32
        )
        rounded = lax.optimization_barrier(partial_value.astype(jnp.bfloat16)).astype(jnp.float32)
        rhs_block = lax.dynamic_index_in_dim(own_rhs, local_block, 1, keepdims=False)
        inverse = lax.dynamic_index_in_dim(inverses, local_block, 0, keepdims=False)
        rhs_full = lax.dynamic_update_slice(
            jnp.zeros((walker_total, block_width), jnp.float32),
            rhs_block,
            (walker_start, jnp.int32(0)),
        )
        term = lax.dot_general(
            rhs_full - rounded,
            inverse,
            (((1,), (1,)), ((), ())),
            precision=lax.Precision.HIGHEST,
            preferred_element_type=jnp.float32,
        )
        term = jnp.where(owns, term, 0.0)
        pair_solution = lax.psum(term, ("row", "col"))
        own_part = lax.dynamic_slice_in_dim(pair_solution, walker_start, slice_width, 0)
        pair_rounded = pair_solution.astype(jnp.bfloat16)
        own_block = jnp.where(is_second, own_part[:, block_width:], own_part[:, :block_width])
        updated = lax.dynamic_update_index_in_dim(solved_local, own_block, local_block, 1)
        solved_local = jnp.where(owns, updated, solved_local)
        for half in range(2):
            block_index = first_block + half
            placed = pair_rounded[:, half * block_width : (half + 1) * block_width]
            known_blocks = jnp.where(my_col == block_index % col_count, placed, known_blocks)
        return (known_blocks, solved_local)

    known_blocks, solved_local = lax.fori_loop(0, pair_total, one_pair, (known_start, solved_start))
    trail_factor = flat_factor[diag_blocks:]
    trail_summed = lax.psum_scatter(
        lax.dot_general(
            known_blocks, trail_factor, (((1,), (2,)), ((), ())), preferred_element_type=jnp.float32
        ).astype(jnp.bfloat16),
        "col",
        scatter_dimension=0,
        tiled=True,
    ).astype(jnp.float32)
    trailing = own_rhs[:, diag_blocks:, :] - trail_summed
    return (solved_local[:, :, None, :], trailing[:, :, None, :])


def solution(mesh):
    placed = (
        P("row", None, None, "col", None, None),
        P("row", None, None, None),
        P("row", None, None, "col"),
    )
    return jax.shard_map(
        shards,
        mesh=mesh,
        in_specs=placed,
        out_specs=(P("col", None, "row", None), P("col", None, "row", None)),
        check_vma=False,
    )
```

profile of v0, /device:TPU:0, one launch (start us, length us, event | category | flops | bytes accessed | tf_op | source)
XLA Modules:
  0.0 657.8 jit_solution(17106109122414137565)
XLA Ops:
  8.0 1.9 copy.40
  11.1 12.1 %all_to_all.27 = bf16[4,2,24576]{2,1,0:T(2,128)(2,1)S(1)} all-to-all(bf16[4,2,24576]{2,1,0:T(2,128)(2,1)S(1)} %reshape.16), channel_id=1, replica_groups=mesh['row'=4,'col'=8] {'row'}, dimensions={0} | all-to-all | bytes 786432 | tf_op jit(solution)/shard_map/all_to_all | solution.py:20
  25.1 4.9 all-to-all-start.1
  29.9 12.6 %all-to-all-done.1 = bf16[8,2,12288]{2,1,0:T(2,128)(2,1)S(1)} async-done(((bf16[8,2,12288]{2,1,0:T(2,128)(2,1)}), bf16[8,2,12288]{2,1,0:T(2,128)(2,1)S(1)}, u32[]{:S(2)}, u32[]{:S(2)}) %all-to-all-start.1) | async-done | bytes 393248 | tf_op jit(solution)/shard_map/all_to_all | solution.py:19
  45.0 560.8 %while.19 = (s32[]{:T(128)}, bf16[256,512]{1,0:T(8,128)(2,1)S(1)}, f32[32,2,512]{2,0,1:T(8,128)S(1)}, s32[]{:T(128)}, s32[]{:T(128)}, /*index=5*/f32[32,12,512]{...) while((s32[]{:T(128)}, bf16[256,512]{1,0:T(8,128)(2,1)S(1)}, ...), condition=%wide.region_2.3_spmd.clone, body=%wide.region_0.2_spmd.clone.sunk | while | flops 1746567168 | bytes 15074070 | solution.py:75
  45.3 1.4 fusion.33
  46.7 1.9 dynamic_update_slice.17
  48.6 6.1 fusion.34
  54.8 126.8 %all-reduce.2.cloned.1.call-done = f32[256,1024]{1,0:T(8,128)} async-done(((f32[256,1024]{1,0:T(8,128)}), f32[256,1024]{1,0:T(8,128)}) %all-reduce.2.cloned.1.call-update) | async-done | bytes 1048592 | tf_op jit(solution)/shard_map/while/body/eval_jaxpr/psum | solution.py:63
  184.3 1.4 fusion.33
  185.7 1.9 dynamic_update_slice.17
  187.7 6.1 fusion.34
  193.9 128.4 %all-reduce.2.cloned.1.call-done = f32[256,1024]{1,0:T(8,128)} async-done(((f32[256,1024]{1,0:T(8,128)}), f32[256,1024]{1,0:T(8,128)}) %all-reduce.2.cloned.1.call-update) | async-done | bytes 1048592 | tf_op jit(solution)/shard_map/while/body/eval_jaxpr/psum | solution.py:63
  324.9 1.4 fusion.33
  326.3 1.9 dynamic_update_slice.17
  328.3 6.1 fusion.34
  334.5 128.4 %all-reduce.2.cloned.1.call-done = f32[256,1024]{1,0:T(8,128)} async-done(((f32[256,1024]{1,0:T(8,128)}), f32[256,1024]{1,0:T(8,128)}) %all-reduce.2.cloned.1.call-update) | async-done | bytes 1048592 | tf_op jit(solution)/shard_map/while/body/eval_jaxpr/psum | solution.py:63
  465.5 1.4 fusion.33
  467.0 1.9 dynamic_update_slice.17
  468.9 6.1 fusion.34
  475.1 128.4 %all-reduce.2.cloned.1.call-done = f32[256,1024]{1,0:T(8,128)} async-done(((f32[256,1024]{1,0:T(8,128)}), f32[256,1024]{1,0:T(8,128)}) %all-reduce.2.cloned.1.call-update) | async-done | bytes 1048592 | tf_op jit(solution)/shard_map/while/body/eval_jaxpr/psum | solution.py:63
  605.9 5.6 fusion.20
  612.3 35.8 %reduce-scatter.2.cloned.1.call-done = bf16[32,10,512]{2,0,1:T(8,128)(2,1)} async-done(((bf16[256,10,512]{2,0,1:T(8,128)(2,1)}), bf16[32,10,512]{2,0,1:T(8,128)(2,1)}) %reduce-scatter.2.cloned.1.call-update) | async-done | bytes 327696 | tf_op jit(solution)/shard_map/reduce_scatter | solution.py:77
  649.2 1.5 copy.34
  (47 shorter events, 17.7 us)
Async XLA Ops:
  25.1 17.4 %all-to-all-start.1 = ((bf16[8,2,12288]{2,1,0:T(2,128)(2,1)}), bf16[8,2,12288]{2,1,0:T(2,128)(2,1)S(1)}, u32[]{:S(2)}, u32[]{:S(2)}) async-start(bf16[8,2,12288]{2,1,0:T(2,128)(2,1)} %reshape.18), calls=%async_computation.1 | async-start | bytes 786432 | tf_op jit(solution)/shard_map/all_to_all | solution.py:19
  45.0 136.6 %all-reduce.2.cloned.1.call-start = ((), (), s32[]{:S(2)}) async-start(), calls=%async_computation.4 | async-start | bytes 2097152 | tf_op jit(solution)/shard_map/while/body/eval_jaxpr/psum | solution.py:63
  184.0 138.2 %all-reduce.2.cloned.1.call-start = ((), (), s32[]{:S(2)}) async-start(), calls=%async_computation.4 | async-start | bytes 2097152 | tf_op jit(solution)/shard_map/while/body/eval_jaxpr/psum | solution.py:63
  324.7 138.2 %all-reduce.2.cloned.1.call-start = ((), (), s32[]{:S(2)}) async-start(), calls=%async_computation.4 | async-start | bytes 2097152 | tf_op jit(solution)/shard_map/while/body/eval_jaxpr/psum | solution.py:63
  465.3 138.2 %all-reduce.2.cloned.1.call-start = ((), (), s32[]{:S(2)}) async-start(), calls=%async_computation.4 | async-start | bytes 2097152 | tf_op jit(solution)/shard_map/while/body/eval_jaxpr/psum | solution.py:63
  605.9 42.2 %reduce-scatter.2.cloned.1.call-start = ((), (), s32[]{:S(2)}) async-start(), calls=%async_computation.3 | async-start | bytes 2949120 | tf_op jit(solution)/shard_map/reduce_scatter | solution.py:77
Sparse Core Ops, SparseCore 0:
  54.9 126.7 all-reduce.1
  193.9 128.3 all-reduce.1
  334.5 128.3 all-reduce.1
  475.1 128.3 all-reduce.1
Sparse Core Ops, SparseCore 1:
  611.6 36.5 reduce-scatter.1
where the time goes:
time: 659 us; the launch traced here: 658 us
  waiting for transfers between devices  561 us (85%)
  matrix products  35.5 us (5%)
  local copies, waits for them, and re-layouts  17.9 us (3%)
  between operations  15.2 us (2%)
  blocking collectives  12.1 us (2%)
  other arithmetic  10.6 us (2%)
    psum x4, waiting for transfers between devices, one_pair(): pair_solution = lax.psum(term, ('row', 'col'))  512 us
    reduce_scatter x1, waiting for transfers between devices, shards(): lax.psum_scatter(lax.dot_general(known_blocks, trail_factor, (((1,), (2,)...  35.8 us
    dot_general x4, matrix products, one_pair(): lax.dot_general(rhs_full - rounded, inverse, (((1,), (1,)), ((), ())), pr...  24.5 us
  transfers between devices with their start and end apart: 6, of which 6 were waited for; matrix products, arithmetic and copies ran while one was open for 0% of the time, Pallas kernels for 0%

commit v1 on v0

v1 whole, which is shorter than its diff:
```python
import functools

import jax
import jax.numpy as jnp
from jax import lax
from jax.experimental import pallas as pl
from jax.experimental.pallas import tpu as pltpu
from jax.sharding import PartitionSpec as P

MESH = pl.DeviceIdType.MESH
NT = (((1,), (1,)), ((), ()))


def dot_nt(x, w):
    return lax.dot_general(x, w, NT, preferred_element_type=jnp.float32)


def kernel(
    n_r,
    n_g,
    factor,
    inv,
    rhs,
    solved,
    trailing,
    lbuf,
    inv_hi,
    inv_lo,
    t_send,
    t_recv,
    y_send,
    ybuf,
    p_send,
    p_recv,
    s_l_own,
    s_l_send,
    s_l_recv,
    s_t_send,
    s_t_recv,
    s_y_send,
    s_y_recv,
    s_p_send,
    s_p_recv,
):
    p = lax.axis_index("row")
    q = lax.axis_index("col")
    g = q // 2
    c = q % 2
    n_a = rhs.shape[0]
    n_d = inv.shape[0]
    sw = rhs.shape[1]
    nb = rhs.shape[2]

    barrier = pltpu.get_barrier_semaphore()

    def greet(i, carry):
        pi, gi = i // n_g, i % n_g

        @pl.when(jnp.logical_or(pi != p, gi != g))
        def _():
            pl.semaphore_signal(
                barrier, inc=1, device_id=(pi, 2 * gi + c), device_id_type=MESH
            )

        return carry

    lax.fori_loop(0, n_r * n_g, greet, 0)
    pl.semaphore_signal(barrier, inc=1, device_id=(p, 2 * g + 1 - c), device_id_type=MESH)
    pl.semaphore_wait(barrier, n_r * n_g)

    def below(a):
        return (a * n_r + p) // 2 > g

    def l_own(a):
        return pltpu.make_async_copy(factor.at[a], lbuf.at[a, c], s_l_own.at[a])

    def l_other(a):
        return pltpu.make_async_remote_copy(
            src_ref=factor.at[a],
            dst_ref=lbuf.at[a, c],
            send_sem=s_l_send.at[a],
            recv_sem=s_l_recv.at[a],
            device_id=(p, 2 * g + 1 - c),
            device_id_type=MESH,
        )

    def l_arrived(a):
        return pltpu.make_async_remote_copy(
            src_ref=factor.at[a],
            dst_ref=lbuf.at[a, 1 - c],
            send_sem=s_l_send.at[a],
            recv_sem=s_l_recv.at[a],
            device_id=(p, 2 * g + 1 - c),
            device_id_type=MESH,
        )

    def l_start(a, carry):
        @pl.when(below(a))
        def _():
            l_own(a).start()
            l_other(a).start()

        return carry

    lax.fori_loop(0, n_a, l_start, 0)

    def split(d, carry):
        full = inv[d]
        hi = full.astype(jnp.bfloat16)
        inv_hi[d] = hi
        inv_lo[d] = (full - hi.astype(jnp.float32)).astype(jnp.bfloat16)
        return carry

    lax.fori_loop(0, n_d, split, 0)

    def part_copy(a, slot, to, at):
        return pltpu.make_async_remote_copy(
            src_ref=p_send.at[a, to],
            dst_ref=p_recv.at[a, slot],
            send_sem=s_p_send.at[a, to],
            recv_sem=s_p_recv.at[a, slot],
            device_id=(p, 2 * at + c),
            device_id_type=MESH,
        )

    def summed(a, count):
        def add(j, total):
            @pl.when(j != g)
            def _():
                part_copy(a, j, j, j).wait_recv()

            return total + p_recv[a, j].astype(jnp.float32)

        return lax.fori_loop(0, count, add, jnp.zeros((sw, nb), jnp.float32))

    def push(a, carry):
        @pl.when(below(a))
        def _():
            l_own(a).wait()
            l_arrived(a).wait_recv()
            x0 = ybuf[0].reshape(n_g * sw, nb)
            x1 = ybuf[1].reshape(n_g * sw, nb)
            part = dot_nt(x0, lbuf[a, 0]) + dot_nt(x1, lbuf[a, 1])
            p_send[a] = part.astype(jnp.bfloat16).reshape(n_g, sw, nb)
            for j in range(n_g):

                @pl.when(g != j)
                def _():
                    part_copy(a, g, j, j).start()

            p_recv[a, g] = p_send[a, g]

        return carry

    def t_copy(d, first):
        second = p - first
        return pltpu.make_async_remote_copy(
            src_ref=t_send.at[d],
            dst_ref=t_recv.at[d],
            send_sem=s_t_send.at[d],
            recv_sem=s_t_recv.at[d],
            device_id=(first + 1 - second, q),
            device_id_type=MESH,
        )

    def y_copy(d, second, m, to):
        return pltpu.make_async_remote_copy(
            src_ref=y_send.at[d],
            dst_ref=ybuf.at[second, g],
            send_sem=s_y_send.at[d, to],
            recv_sem=s_y_recv.at[second, g],
            device_id=(to, 2 * m + c),
            device_id_type=MESH,
        )

    def y_arrived(second, j):
        return pltpu.make_async_remote_copy(
            src_ref=y_send.at[0],
            dst_ref=ybuf.at[second, j],
            send_sem=s_y_send.at[0, 0],
            recv_sem=s_y_recv.at[second, j],
            device_id=(p, q),
            device_id_type=MESH,
        )

    def one_pair(m, carry):
        d = (2 * m) // n_r
        first = (2 * m) % n_r
        second = p - first
        owns = jnp.logical_or(p == first, p == first + 1)

        @pl.when(owns)
        def _():
            diff = rhs[d].astype(jnp.float32) - summed(d, m)
            hi = diff.astype(jnp.bfloat16)
            lo = (diff - hi.astype(jnp.float32)).astype(jnp.bfloat16)
            both = jnp.concatenate([hi, lo], axis=0)

            def half(start):
                rows = pl.ds(pl.multiple_of(start, nb), nb)
                wide = dot_nt(both, inv_hi[d, rows])
                return wide[:sw] + wide[sw:] + dot_nt(hi, inv_lo[d, rows])

            t_send[d] = half((1 - second) * nb)
            t_copy(d, first).start()
            mine = half(second * nb)
            t_copy(d, first).wait_recv()
            value = mine + t_recv[d]
            y_send[d] = value.astype(jnp.bfloat16)
            for to in range(n_r):

                @pl.when(jnp.logical_or(to != p, m != g))
                def _():
                    y_copy(d, second, m, to).start()

            solved[d] = value

            @pl.when(m == g)
            def _():
                ybuf[second, g] = y_send[d]

        @pl.when(m == g)
        def _():
            for j in range(n_g):
                for s in range(2):

                    @pl.when(jnp.logical_or(j != g, p != first + s))
                    def _():
                        y_arrived(s, j).wait_recv()

            lax.fori_loop(0, n_d, push, 0)

        @pl.when(m == g + 1)
        def _():
            lax.fori_loop(n_d, n_a, push, 0)

        return carry

    lax.fori_loop(0, n_g, one_pair, 0)

    @pl.when(g == n_g - 1)
    def _():
        lax.fori_loop(n_d, n_a, push, 0)

    def finish(a, carry):
        trailing[a - n_d] = rhs[a].astype(jnp.float32) - summed(a, n_g)
        return carry

    lax.fori_loop(n_d, n_a, finish, 0)

    def drain_pair(m, carry):
        d = (2 * m) // n_r
        first = (2 * m) % n_r
        second = p - first

        @pl.when(jnp.logical_or(p == first, p == first + 1))
        def _():
            t_copy(d, first).wait_send()
            for to in range(n_r):

                @pl.when(jnp.logical_or(to != p, m != g))
                def _():
                    y_copy(d, second, m, to).wait_send()

        return carry

    lax.fori_loop(0, n_g, drain_pair, 0)

    def drain_rows(a, carry):
        @pl.when(below(a))
        def _():
            l_other(a).wait_send()
            for j in range(n_g):

                @pl.when(g != j)
                def _():
                    part_copy(a, g, j, j).wait_send()

        return carry

    lax.fori_loop(0, n_a, drain_rows, 0)


def shards(factor, diag_inverse, residuals):
    n_r = lax.axis_size("row")
    n_col = lax.axis_size("col")
    n_g = n_col // 2
    flat = factor[0, :, :, 0, 0, :]
    n_a, nb = flat.shape[0], flat.shape[1]
    inverses = diag_inverse[0]
    n_d = inverses.shape[0]
    relaid = lax.all_to_all(
        lax.all_to_all(
            residuals.astype(jnp.bfloat16), "row", split_axis=2, concat_axis=0, tiled=True
        ),
        "col",
        split_axis=0,
        concat_axis=3,
        tiled=True,
    )
    rhs = relaid[:, :, 0, :].transpose(1, 0, 2)
    sw = rhs.shape[1]
    bf, f32 = jnp.bfloat16, jnp.float32
    vmem = pl.BlockSpec(memory_space=pltpu.VMEM)
    dma = pltpu.SemaphoreType.DMA
    solved, trailing = pl.pallas_call(
        functools.partial(kernel, n_r, n_g),
        out_shape=(
            jax.ShapeDtypeStruct((n_d, sw, nb), f32),
            jax.ShapeDtypeStruct((n_a - n_d, sw, nb), f32),
        ),
        in_specs=[pl.BlockSpec(memory_space=pl.ANY), vmem, vmem],
        out_specs=(vmem, vmem),
        scratch_shapes=[
            pltpu.VMEM((n_a, 2, nb, nb), bf),
            pltpu.VMEM(inverses.shape, bf),
            pltpu.VMEM(inverses.shape, bf),
            pltpu.VMEM((n_d, sw, nb), f32),
            pltpu.VMEM((n_d, sw, nb), f32),
            pltpu.VMEM((n_d, sw, nb), bf),
            pltpu.VMEM((2, n_g, sw, nb), bf),
            pltpu.VMEM((n_a, n_g, sw, nb), bf),
            pltpu.VMEM((n_a, n_g, sw, nb), bf),
            dma((n_a,)),
            dma((n_a,)),
            dma((n_a,)),
            dma((n_d,)),
            dma((n_d,)),
            dma((n_d, n_r)),
            dma((2, n_g)),
            dma((n_a, n_g)),
            dma((n_a, n_g)),
        ],
        compiler_params=pltpu.CompilerParams(
            collective_id=0, has_side_effects=True, vmem_limit_bytes=48 * 1024 * 1024
        ),
        cost_estimate=pl.CostEstimate(
            flops=2 * n_a * sw * n_g * 2 * nb * nb,
            bytes_accessed=2 * n_a * nb * nb * 2,
            transcendentals=0,
        ),
    )(flat, inverses, rhs)
    return (
        solved.transpose(1, 0, 2)[:, :, None, :],
        trailing.transpose(1, 0, 2)[:, :, None, :],
    )


def solution(mesh):
    placed = (
        P("row", None, None, "col", None, None),
        P("row", None, None, None),
        P("row", None, None, "col"),
    )
    return jax.shard_map(
        shards,
        mesh=mesh,
        in_specs=placed,
        out_specs=(P("col", None, "row", None), P("col", None, "row", None)),
        check_vma=False,
    )
```

time: 659 us -> 124 us (0.19)
  waiting for transfers between devices: 561 us -> 0 us
  Pallas kernels: 0 us -> 82.9 us
  matrix products: 35.5 us -> 0 us
  blocking collectives: 12.1 us -> 29.3 us
  between operations: 15.2 us -> 0.7 us
  other arithmetic: 10.6 us -> 0 us
  local copies, waits for them, and re-layouts: 17.9 us -> 10.3 us
    psum x4 -> x0, waiting for transfers between devices: 512 us -> none  [one_pair(): pair_solution = lax.psum(term, ('row', 'col'))]
    pallas_call x0 -> x1, Pallas kernels: none -> 82.9 us  [shards(): pl.pallas_call(functools.partial(kernel, n_r, n_g), out_shape=(jax.ShapeD...]
    reduce_scatter x1 -> x0, waiting for transfers between devices: 35.8 us -> none  [shards(): lax.psum_scatter(lax.dot_general(known_blocks, trail_factor, (((1,), (2,)...]
    dot_general x9 -> x0, matrix products: 35.5 us -> none  [the longest x4 24.5 us: one_pair(): lax.dot_general(rhs_full - rounded, inverse, (((1,), (1,)), ((), ())), pr...]
    all_to_all x0 -> x1, blocking collectives: none -> 17.2 us  [shards(): lax.all_to_all(lax.all_to_all(residuals.astype(jnp.bfloat16), 'row', spli...]
    all_to_all x1 -> x0, waiting for transfers between devices: 12.6 us -> none  [shards(): lax.all_to_all(lax.all_to_all(residuals.astype(jnp.bfloat16), 'row', spli...]
    dynamic_update_slice x4 -> x0, local copies, waits for them, and re-layouts: 7.68 us -> none  [one_pair(): lax.dynamic_update_slice(jnp.zeros((walker_total, block_width), jnp.float...]
  transfers between devices with their start and end apart: 6 -> 0, of which waited for: 6 -> 0; matrix products, arithmetic and copies ran while one was open for 0% -> 0% of each run, Pallas kernels for 0% -> 0%
where the time goes in v1:
time: 124 us; the launch traced here: 123 us
  Pallas kernels  82.9 us (67%)
  blocking collectives  29.3 us (24%)
  local copies, waits for them, and re-layouts  10.3 us (8%)
    pallas_call x1, Pallas kernels, shards(): pl.pallas_call(functools.partial(kernel, n_r, n_g), out_shape=(jax.ShapeD...  82.9 us
    all_to_all x1, blocking collectives, shards(): lax.all_to_all(lax.all_to_all(residuals.astype(jnp.bfloat16), 'row', spli...  17.2 us
    all_to_all x1, blocking collectives, shards(): lax.all_to_all(residuals.astype(jnp.bfloat16), 'row', split_axis=2, conca...  12.1 us
    unnamed x9, local copies, waits for them, and re-layouts  8.73 us

profile of v1, /device:TPU:0, one launch (start us, length us, event | category | flops | bytes accessed | tf_op | source)
XLA Modules:
  0.0 123.2 jit_solution(8627507927467274288)
XLA Ops:
  0.6 1.9 %copy.30 = bf16[64,12,4,64]{3,0,2,1:T(8,128)(2,1)S(1)} copy(f32[64,12,4,64]{3,2,1,0:T(4,128)} %param.5) | data formatting | bytes 1179648 | tf_op args[2]
  2.5 0.5 copy.32
  3.1 0.6 reshape.5
  3.7 12.1 %all_to_all.33 = bf16[4,2,24576]{2,1,0:T(2,128)(2,1)S(1)} all-to-all(bf16[4,2,24576]{2,1,0:T(2,128)(2,1)S(1)} %reshape.5), channel_id=1, replica_groups=mesh['row'=4,'col'=8] {'row'}, dimensions={0} | all-to-all | bytes 786432 | tf_op jit(solution)/shard_map/all_to_all | solution.py:293
  15.8 0.6 reshape.6
  16.4 0.6 reshape.7
  16.9 17.2 %all_to_all.34 = bf16[8,2,12288]{2,1,0:T(2,128)(2,1)S(1)} all-to-all(bf16[8,2,12288]{2,1,0:T(2,128)(2,1)S(1)} %reshape.7), channel_id=1, replica_groups=mesh['row'=4,'col'=8] {'col'}, dimensions={0} | all-to-all | bytes 786432 | tf_op jit(solution)/shard_map/all_to_all | solution.py:292
  34.2 0.6 reshape.8
  34.8 0.2 copy.23
  35.0 0.3 copy.24
  35.3 0.5 squeeze.11
  35.8 0.0 copy-start
  35.8 2.2 %copy-done = f32[1,2,1024,512]{3,2,1,0:T(8,128)S(1)} copy-done((f32[1,2,1024,512]{3,2,1,0:T(8,128)S(1)}, f32[1,2,1024,512]{3,2,1,0:T(8,128)}, u32[]{:S(2)}) %copy-start) | copy-done | bytes 4194328
  38.0 82.9 %shard_map.50 = (f32[2,32,512]{2,1,0:T(8,128)S(1)}, f32[10,32,512]{2,1,0:T(8,128)S(1)}) custom-call(bf16[12,512,512]{2,1,0:T(8,128)(2,1)} %bitcast.33, f32[2,1024,512]{2,1,0:T(8,128)S(1)} %bitcast.29, bf16[12,32,512]{2,1,0:T(8,128)(2,1)S(1)} %bitcast.30), custom_call_target="tpu_custom_call" | custom-call | flops 1610612736 | bytes 12582912 | tf_op jit(solution)/shard_map/pallas_call | solution.py:306
  120.9 0.8 copy.25
  121.7 1.5 %copy.26 = f32[32,10,1,512]{3,2,1,0:T(1,128)} copy(f32[32,10,1,512]{3,0,1,2:T(8,128)S(1)} %bitcast.31) | data formatting | bytes 1310720
Async XLA Ops:
  35.8 2.2 %copy-start = (f32[1,2,1024,512]{3,2,1,0:T(8,128)S(1)}, f32[1,2,1024,512]{3,2,1,0:T(8,128)}, u32[]{:S(2)}) copy-start(f32[1,2,1024,512]{3,2,1,0:T(8,128)} %param.4) | copy-start | bytes 12582916

commit v2 on v1

--- a/solution.py
+++ b/solution.py
@@ -19,10 +19,13 @@
     n_r,
     n_g,
     factor,
-    inv,
-    rhs,
+    inv_in,
+    packed,
     solved,
     trailing,
+    inv,
+    rbuf,
+    rhs,
     lbuf,
     inv_hi,
     inv_lo,
@@ -32,6 +35,10 @@
     ybuf,
     p_send,
     p_recv,
+    s_inv,
+    s_r_own,
+    s_r_send,
+    s_r_recv,
     s_l_own,
     s_l_send,
     s_l_recv,
@@ -51,22 +58,91 @@
     sw = rhs.shape[1]
     nb = rhs.shape[2]
 
+    n_col = 2 * n_g
+    n_w = packed.shape[0]
+    n_k = packed.shape[2]
+    fold = n_a // n_k
+    lw = nb // n_col
+    n_u = -(-n_d // fold)
+
+    def inv_copy(d):
+        return pltpu.make_async_copy(inv_in.at[d], inv.at[d], s_inv.at[d])
+
+    for d in range(n_d):
+        inv_copy(d).start()
+
     barrier = pltpu.get_barrier_semaphore()
 
     def greet(i, carry):
-        pi, gi = i // n_g, i % n_g
-
-        @pl.when(jnp.logical_or(pi != p, gi != g))
-        def _():
-            pl.semaphore_signal(
-                barrier, inc=1, device_id=(pi, 2 * gi + c), device_id_type=MESH
-            )
-
-        return carry
-
-    lax.fori_loop(0, n_r * n_g, greet, 0)
-    pl.semaphore_signal(barrier, inc=1, device_id=(p, 2 * g + 1 - c), device_id_type=MESH)
-    pl.semaphore_wait(barrier, n_r * n_g)
+        pi, qi = i // n_col, i % n_col
+
+        @pl.when(jnp.logical_or(pi != p, qi != q))
+        def _():
+            pl.semaphore_signal(barrier, inc=1, device_id=(pi, qi), device_id_type=MESH)
+
+        return carry
+
+    lax.fori_loop(0, n_r * n_col, greet, 0)
+    pl.semaphore_wait(barrier, n_r * n_col - 1)
+
+    spans = (pl.ds(0, n_u), pl.ds(n_u, n_k - n_u))
+
+    def r_copy(j, to, part):
+        return pltpu.make_async_remote_copy(
+            src_ref=packed.at[j, to, spans[part]],
+            dst_ref=rbuf.at[q, spans[part]],
+            send_sem=s_r_send.at[j, to, part],
+            recv_sem=s_r_recv.at[q, part],
+            device_id=(to, p * n_w + j),
+            device_id_type=MESH,
+        )
+
+    def r_own(j, part):
+        return pltpu.make_async_copy(
+            packed.at[j, p, spans[part]], rbuf.at[q, spans[part]], s_r_own.at[part]
+        )
+
+    def r_arrived(j, part):
+        return pltpu.make_async_remote_copy(
+            src_ref=packed.at[0, 0, spans[part]],
+            dst_ref=rbuf.at[j, spans[part]],
+            send_sem=s_r_send.at[0, 0, part],
+            recv_sem=s_r_recv.at[j, part],
+            device_id=(p, q),
+            device_id_type=MESH,
+        )
+
+    def r_start(part):
+        for j in range(n_w):
+            for to in range(n_r):
+                here = jnp.logical_and(to == p, p * n_w + j == q)
+
+                @pl.when(here)
+                def _():
+                    r_own(j, part).start()
+
+                @pl.when(jnp.logical_not(here))
+                def _():
+                    r_copy(j, to, part).start()
+
+    def r_wait(part):
+        for j in range(n_col):
+            here = jnp.logical_and(j == q, p == q // n_w)
+
+            @pl.when(here)
+            def _():
+                r_own(q % n_w, part).wait()
+
+            @pl.when(jnp.logical_not(here))
+            def _():
+                r_arrived(j, part).wait_recv()
+
+    def unpack(k, carry):
+        for j in range(n_col):
+            piece = rbuf[j, k].astype(jnp.float32)
+            for s in range(fold):
+                rhs[k * fold + s, :, j * lw : (j + 1) * lw] = piece[:, s * lw : (s + 1) * lw]
+        return carry
 
     def below(a):
         return (a * n_r + p) // 2 > g
@@ -102,16 +178,22 @@
 
         return carry
 
-    lax.fori_loop(0, n_a, l_start, 0)
+    r_start(0)
+    lax.fori_loop(0, n_d, l_start, 0)
+    r_start(1)
+    lax.fori_loop(n_d, n_a, l_start, 0)
 
     def split(d, carry):
+        inv_copy(d).wait()
         full = inv[d]
         hi = full.astype(jnp.bfloat16)
         inv_hi[d] = hi
         inv_lo[d] = (full - hi.astype(jnp.float32)).astype(jnp.bfloat16)
         return carry
 
-    lax.fori_loop(0, n_d, split, 0)
+    split(0, 0)
+    r_wait(0)
+    lax.fori_loop(0, n_u, unpack, 0)
 
     def part_copy(a, slot, to, at):
         return pltpu.make_async_remote_copy(
@@ -191,7 +273,7 @@
 
         @pl.when(owns)
         def _():
-            diff = rhs[d].astype(jnp.float32) - summed(d, m)
+            diff = rhs[d] - summed(d, m)
             hi = diff.astype(jnp.bfloat16)
             lo = (diff - hi.astype(jnp.float32)).astype(jnp.bfloat16)
             both = jnp.concatenate([hi, lo], axis=0)
@@ -230,6 +312,10 @@
 
             lax.fori_loop(0, n_d, push, 0)
 
+        @pl.when(m == 0)
+        def _():
+            lax.fori_loop(1, n_d, split, 0)
+
         @pl.when(m == g + 1)
         def _():
             lax.fori_loop(n_d, n_a, push, 0)
@@ -242,11 +328,22 @@
     def _():
         lax.fori_loop(n_d, n_a, push, 0)
 
+    r_wait(1)
+    lax.fori_loop(n_u, n_k, unpack, 0)
+
     def finish(a, carry):
-        trailing[a - n_d] = rhs[a].astype(jnp.float32) - summed(a, n_g)
+        trailing[a - n_d] = rhs[a] - summed(a, n_g)
         return carry
 
     lax.fori_loop(n_d, n_a, finish, 0)
+
+    for part in range(2):
+        for j in range(n_w):
+            for to in range(n_r):
+
+                @pl.when(jnp.logical_or(to != p, p * n_w + j != q))
+                def _():
+                    r_copy(j, to, part).wait_send()
 
     def drain_pair(m, carry):
         d = (2 * m) // n_r
@@ -289,17 +386,16 @@
     n_a, nb = flat.shape[0], flat.shape[1]
     inverses = diag_inverse[0]
     n_d = inverses.shape[0]
-    relaid = lax.all_to_all(
-        lax.all_to_all(
-            residuals.astype(jnp.bfloat16), "row", split_axis=2, concat_axis=0, tiled=True
-        ),
-        "col",
-        split_axis=0,
-        concat_axis=3,
-        tiled=True,
+    lw = nb // n_col
+    fold = 128 // lw
+    sw = residuals.shape[0] * n_r // n_col
+    n_w = residuals.shape[0] // sw
+    packed = (
+        residuals.astype(jnp.bfloat16)
+        .reshape(n_w, sw, n_a // fold, fold, n_r, lw)
+        .transpose(0, 4, 2, 1, 3, 5)
+        .reshape(n_w, n_r, n_a // fold, sw, fold * lw)
     )
-    rhs = relaid[:, :, 0, :].transpose(1, 0, 2)
-    sw = rhs.shape[1]
     bf, f32 = jnp.bfloat16, jnp.float32
     vmem = pl.BlockSpec(memory_space=pltpu.VMEM)
     dma = pltpu.SemaphoreType.DMA
@@ -309,9 +405,12 @@
             jax.ShapeDtypeStruct((n_d, sw, nb), f32),
             jax.ShapeDtypeStruct((n_a - n_d, sw, nb), f32),
         ),
-        in_specs=[pl.BlockSpec(memory_space=pl.ANY), vmem, vmem],
+        in_specs=[pl.BlockSpec(memory_space=pl.ANY)] * 3,
         out_specs=(vmem, vmem),
         scratch_shapes=[
+            pltpu.VMEM(inverses.shape, f32),
+            pltpu.VMEM((n_col, n_a // fold, sw, fold * lw), bf),
+            pltpu.VMEM((n_a, sw, nb), f32),
             pltpu.VMEM((n_a, 2, nb, nb), bf),
             pltpu.VMEM(inverses.shape, bf),
             pltpu.VMEM(inverses.shape, bf),
@@ -321,6 +420,10 @@
             pltpu.VMEM((2, n_g, sw, nb), bf),
             pltpu.VMEM((n_a, n_g, sw, nb), bf),
             pltpu.VMEM((n_a, n_g, sw, nb), bf),
+            dma((n_d,)),
+            dma((2,)),
+            dma((n_w, n_r, 2)),
+            dma((n_col, 2)),
             dma((n_a,)),
             dma((n_a,)),
             dma((n_a,)),
@@ -332,14 +435,14 @@
             dma((n_a, n_g)),
         ],
         compiler_params=pltpu.CompilerParams(
-            collective_id=0, has_side_effects=True, vmem_limit_bytes=48 * 1024 * 1024
+            collective_id=0, has_side_effects=True, vmem_limit_bytes=60 * 1024 * 1024
         ),
         cost_estimate=pl.CostEstimate(
             flops=2 * n_a * sw * n_g * 2 * nb * nb,
             bytes_accessed=2 * n_a * nb * nb * 2,
             transcendentals=0,
         ),
-    )(flat, inverses, rhs)
+    )(flat, inverses, packed)
     return (
         solved.transpose(1, 0, 2)[:, :, None, :],
         trailing.transpose(1, 0, 2)[:, :, None, :],

time: 124 us -> 123 us (level)
  Pallas kernels: 82.9 us -> 114 us
  blocking collectives: 29.3 us -> 0 us
  local copies, waits for them, and re-layouts: 10.3 us -> 6.25 us
  other arithmetic: 0 us -> 1.68 us
    pallas_call x1, Pallas kernels: 82.9 us -> 114 us  [shards(): pl.pallas_call(functools.partial(kernel, n_r, n_g), out_shape=(jax.ShapeD...]
    all_to_all x2 -> x0, blocking collectives: 29.3 us -> none  [the longest x1 17.2 us: shards(): lax.all_to_all(lax.all_to_all(residuals.astype(jnp.bfloat16), 'row', spli...]
    unnamed x9 -> x2, local copies, waits for them, and re-layouts: 8.73 us -> 4.29 us
    reshape x0 -> x2, local copies, waits for them, and re-layouts: none -> 1.95 us  [shards(): packed = residuals.astype(jnp.bfloat16).reshape(n_w, sw, n_a // fold, fol...]
    convert_element_type x0 -> x1, other arithmetic: none -> 1.68 us  [shards(): residuals.astype(jnp.bfloat16).reshape(n_w, sw, n_a // fold, fold, n_r, lw)]
where the time goes in v2:
time: 123 us
  Pallas kernels  114 us (93%)
  local copies, waits for them, and re-layouts  6.25 us (5%)
  other arithmetic  1.68 us (1%)
    pallas_call x1, Pallas kernels, shards(): pl.pallas_call(functools.partial(kernel, n_r, n_g), out_shape=(jax.ShapeD...  114 us
    unnamed x2, local copies, waits for them, and re-layouts  4.29 us

profile of v2, /device:TPU:0, one launch (start us, length us, event | category | flops | bytes accessed | tf_op | source)
XLA Modules:
  0.0 122.7 jit_solution(14288117107858536804)
XLA Ops:
  0.6 1.7 %convert_element_type.3 = bf16[64,12,4,64]{3,2,1,0:T(4,128)(2,1)S(1)} convert(f32[64,12,4,64]{3,2,1,0:T(4,128)} %param.5) | non-fusion elementwise | flops 196608 | bytes 1179648 | tf_op jit(solution)/shard_map/convert_element_type | solution.py:394
  2.3 0.9 copy.9
  3.2 1.1 reshape.11.packed
  4.3 114.2 %shard_map.50 = (f32[2,32,512]{2,1,0:T(8,128)}, f32[10,32,512]{2,1,0:T(8,128)}) custom-call(bf16[12,512,512]{2,1,0:T(8,128)(2,1)} %bitcast.12, f32[2,1024,512]{2,1,0:T(8,128)} %bitcast.13, bf16[2,4,6,32,128]{4,3,2,1,0:T(8,128)(2,1)} %reshape.11.packed), custom_call_target="tpu_custom_call" | custom-call | flops 1610612736 | bytes 12582912 | tf_op jit(solution)/shard_map/pallas_call | solution.py:402
  118.5 1.7 %copy.6 = f32[32,2,1,512]{3,2,1,0:T(1,128)} copy(f32[32,2,1,512]{3,0,1,2:T(8,128)} %bitcast.17) | data formatting | bytes 262144
  120.1 2.6 %copy.7 = f32[32,10,1,512]{3,2,1,0:T(1,128)} copy(f32[32,10,1,512]{3,0,1,2:T(8,128)} %bitcast.16) | data formatting | bytes 1310720

commit v3 on v2

--- a/solution.py
+++ b/solution.py
@@ -24,6 +24,7 @@
     solved,
     trailing,
     inv,
+    mid,
     rbuf,
     rhs,
     lbuf,
@@ -39,6 +40,9 @@
     s_r_own,
     s_r_send,
     s_r_recv,
+    s_m_own,
+    s_m_send,
+    s_m_recv,
     s_l_own,
     s_l_send,
     s_l_recv,
@@ -87,51 +91,112 @@
 
     spans = (pl.ds(0, n_u), pl.ds(n_u, n_k - n_u))
 
-    def r_copy(j, to, part):
-        return pltpu.make_async_remote_copy(
-            src_ref=packed.at[j, to, spans[part]],
-            dst_ref=rbuf.at[q, spans[part]],
-            send_sem=s_r_send.at[j, to, part],
-            recv_sem=s_r_recv.at[q, part],
+    def r_here(j, to):
+        return jnp.logical_and(to == p, p * n_w + j == q)
+
+    def r_copy(j, to):
+        return pltpu.make_async_remote_copy(
+            src_ref=packed.at[j, to, spans[0]],
+            dst_ref=rbuf.at[q, spans[0]],
+            send_sem=s_r_send.at[j * n_r + to, 0],
+            recv_sem=s_r_recv.at[q, 0],
             device_id=(to, p * n_w + j),
             device_id_type=MESH,
         )
 
-    def r_own(j, part):
-        return pltpu.make_async_copy(
-            packed.at[j, p, spans[part]], rbuf.at[q, spans[part]], s_r_own.at[part]
-        )
+    def r_own(part):
+        src = packed.at[q % n_w, p, spans[0]] if part == 0 else mid.at[q // n_w, q % n_w]
+        return pltpu.make_async_copy(src, rbuf.at[q, spans[part]], s_r_own.at[part])
 
     def r_arrived(j, part):
         return pltpu.make_async_remote_copy(
             src_ref=packed.at[0, 0, spans[part]],
             dst_ref=rbuf.at[j, spans[part]],
-            send_sem=s_r_send.at[0, 0, part],
+            send_sem=s_r_send.at[0, part],
             recv_sem=s_r_recv.at[j, part],
             device_id=(p, q),
             device_id_type=MESH,
         )
 
-    def r_start(part):
+    def m_own():
+        return pltpu.make_async_copy(packed.at[:, p, spans[1]], mid.at[p], s_m_own)
+
+    def m_copy(to):
+        return pltpu.make_async_remote_copy(
+            src_ref=packed.at[:, to, spans[1]],
+            dst_ref=mid.at[p],
+            send_sem=s_m_send.at[to],
+            recv_sem=s_m_recv.at[p],
+            device_id=(to, q),
+            device_id_type=MESH,
+        )
+
+    def m_arrived(j):
+        return pltpu.make_async_remote_copy(
+            src_ref=packed.at[:, 0, spans[1]],
+            dst_ref=mid.at[j],
+            send_sem=s_m_send.at[0],
+            recv_sem=s_m_recv.at[j],
+            device_id=(p, q),
+            device_id_type=MESH,
+        )
+
+    def m_relay(to):
+        return pltpu.make_async_remote_copy(
+            src_ref=mid.at[to // n_w, to % n_w],
+            dst_ref=rbuf.at[q, spans[1]],
+            send_sem=s_r_send.at[to, 1],
+            recv_sem=s_r_recv.at[q, 1],
+            device_id=(p, to),
+            device_id_type=MESH,
+        )
+
+    def r_start():
         for j in range(n_w):
             for to in range(n_r):
-                here = jnp.logical_and(to == p, p * n_w + j == q)
-
-                @pl.when(here)
+
+                @pl.when(jnp.logical_not(r_here(j, to)))
                 def _():
-                    r_own(j, part).start()
-
-                @pl.when(jnp.logical_not(here))
-                def _():
-                    r_copy(j, to, part).start()
+                    r_copy(j, to).start()
+
+        @pl.when(p == q // n_w)
+        def _():
+            r_own(0).start()
+
+    def m_start():
+        for to in range(n_r):
+
+            @pl.when(to != p)
+            def _():
+                m_copy(to).start()
+
+        m_own().start()
+
+    def relay():
+        m_own().wait()
+        for j in range(n_r):
+
+            @pl.when(j != p)
+            def _():
+                m_arrived(j).wait_recv()
+
+        for j in range(n_col):
+
+            @pl.when(j != q)
+            def _():
+                m_relay(j).start()
+
+        r_own(1).start()
 
     def r_wait(part):
         for j in range(n_col):
-            here = jnp.logical_and(j == q, p == q // n_w)
+            here = j == q
+            if part == 0:
+                here = jnp.logical_and(here, p == q // n_w)
 
             @pl.when(here)
             def _():
-                r_own(q % n_w, part).wait()
+                r_own(part).wait()
 
             @pl.when(jnp.logical_not(here))
             def _():
@@ -178,9 +243,9 @@
 
         return carry
 
-    r_start(0)
+    r_start()
     lax.fori_loop(0, n_d, l_start, 0)
-    r_start(1)
+    m_start()
     lax.fori_loop(n_d, n_a, l_start, 0)
 
     def split(d, carry):
@@ -322,6 +387,7 @@
 
         return carry
 
+    relay()
     lax.fori_loop(0, n_g, one_pair, 0)
 
     @pl.when(g == n_g - 1)
@@ -337,13 +403,24 @@
 
     lax.fori_loop(n_d, n_a, finish, 0)
 
-    for part in range(2):
-        for j in range(n_w):
-            for to in range(n_r):
-
-                @pl.when(jnp.logical_or(to != p, p * n_w + j != q))
-                def _():
-                    r_copy(j, to, part).wait_send()
+    for j in range(n_w):
+        for to in range(n_r):
+
+            @pl.when(jnp.logical_not(r_here(j, to)))
+            def _():
+                r_copy(j, to).wait_send()
+
+    for j in range(n_r):
+
+        @pl.when(j != p)
+        def _():
+            m_copy(j).wait_send()
+
+    for j in range(n_col):
+
+        @pl.when(j != q)
+        def _():
+            m_relay(j).wait_send()
 
     def drain_pair(m, carry):
         d = (2 * m) // n_r
@@ -388,6 +465,7 @@
     n_d = inverses.shape[0]
     lw = nb // n_col
     fold = 128 // lw
+    n_u = -(-n_d // fold)
     sw = residuals.shape[0] * n_r // n_col
     n_w = residuals.shape[0] // sw
     packed = (
@@ -409,6 +487,7 @@
         out_specs=(vmem, vmem),
         scratch_shapes=[
             pltpu.VMEM(inverses.shape, f32),
+            pltpu.VMEM((n_r, n_w, n_a // fold - n_u, sw, fold * lw), bf),
             pltpu.VMEM((n_col, n_a // fold, sw, fold * lw), bf),
             pltpu.VMEM((n_a, sw, nb), f32),
             pltpu.VMEM((n_a, 2, nb, nb), bf),
@@ -422,8 +501,11 @@
             pltpu.VMEM((n_a, n_g, sw, nb), bf),
             dma((n_d,)),
             dma((2,)),
-            dma((n_w, n_r, 2)),
             dma((n_col, 2)),
+            dma((n_col, 2)),
+            dma,
+            dma((n_r,)),
+            dma((n_r,)),
             dma((n_a,)),
             dma((n_a,)),
             dma((n_a,)),

time: 123 us -> 109 us (0.89)
  Pallas kernels: 114 us -> 99.7 us
    pallas_call x1, Pallas kernels: 114 us -> 99.7 us  [shards(): pl.pallas_call(functools.partial(kernel, n_r, n_g), out_shape=(jax.ShapeD...]
where the time goes in v3:
time: 109 us; the launch traced here: 108 us
  Pallas kernels  99.7 us (91%)
  local copies, waits for them, and re-layouts  6.25 us (6%)
  other arithmetic  1.68 us (2%)
    pallas_call x1, Pallas kernels, shards(): pl.pallas_call(functools.partial(kernel, n_r, n_g), out_shape=(jax.ShapeD...  99.7 us
    unnamed x2, local copies, waits for them, and re-layouts  4.29 us

profile of v3, /device:TPU:0, one launch (start us, length us, event | category | flops | bytes accessed | tf_op | source)
XLA Modules:
  0.0 108.3 jit_solution(7159716555431213718)
XLA Ops:
  0.6 1.7 %convert_element_type.3 = bf16[64,12,4,64]{3,2,1,0:T(4,128)(2,1)S(1)} convert(f32[64,12,4,64]{3,2,1,0:T(4,128)} %param.5) | non-fusion elementwise | flops 196608 | bytes 1179648 | tf_op jit(solution)/shard_map/convert_element_type | solution.py:472
  2.3 0.9 copy.9
  3.2 1.1 %reshape.11.packed = bf16[2,4,6,32,128]{4,3,2,1,0:T(8,128)(2,1)} reshape(bf16[2,4,6,32,2,64]{5,4,3,2,1,0:T(2,128)(2,1)S(1)} %bitcast.14) | data formatting | bytes 786432 | tf_op jit(solution)/shard_map/reshape | solution.py:475
  4.3 99.7 %shard_map.50 = (f32[2,32,512]{2,1,0:T(8,128)}, f32[10,32,512]{2,1,0:T(8,128)}) custom-call(bf16[12,512,512]{2,1,0:T(8,128)(2,1)} %bitcast.12, f32[2,1024,512]{2,1,0:T(8,128)} %bitcast.13, bf16[2,4,6,32,128]{4,3,2,1,0:T(8,128)(2,1)} %reshape.11.packed), custom_call_target="tpu_custom_call" | custom-call | flops 1610612736 | bytes 12582912 | tf_op jit(solution)/shard_map/pallas_call | solution.py:480
  104.0 1.7 %copy.6 = f32[32,2,1,512]{3,2,1,0:T(1,128)} copy(f32[32,2,1,512]{3,0,1,2:T(8,128)} %bitcast.17) | data formatting | bytes 262144
  105.7 2.6 %copy.7 = f32[32,10,1,512]{3,2,1,0:T(1,128)} copy(f32[32,10,1,512]{3,0,1,2:T(8,128)} %bitcast.16) | data formatting | bytes 1310720

commit v4 on v3

--- a/solution.py
+++ b/solution.py
@@ -50,6 +50,7 @@
     s_t_recv,
     s_y_send,
     s_y_recv,
+    s_y_pass,
     s_p_send,
     s_p_recv,
 ):
@@ -256,6 +257,7 @@
         inv_lo[d] = (full - hi.astype(jnp.float32)).astype(jnp.bfloat16)
         return carry
 
+    relay()
     split(0, 0)
     r_wait(0)
     lax.fori_loop(0, n_u, unpack, 0)
@@ -320,6 +322,16 @@
             device_id_type=MESH,
         )
 
+    def y_pass(second, j, to):
+        return pltpu.make_async_remote_copy(
+            src_ref=ybuf.at[second, j],
+            dst_ref=ybuf.at[second, j],
+            send_sem=s_y_pass.at[j, to],
+            recv_sem=s_y_recv.at[second, j],
+            device_id=(to, q),
+            device_id_type=MESH,
+        )
+
     def y_arrived(second, j):
         return pltpu.make_async_remote_copy(
             src_ref=y_send.at[0],
@@ -354,11 +366,10 @@
             t_copy(d, first).wait_recv()
             value = mine + t_recv[d]
             y_send[d] = value.astype(jnp.bfloat16)
-            for to in range(n_r):
-
-                @pl.when(jnp.logical_or(to != p, m != g))
-                def _():
-                    y_copy(d, second, m, to).start()
+
+            @pl.when(m != g)
+            def _():
+                y_copy(d, second, m, p).start()
 
             solved[d] = value
 
@@ -368,10 +379,22 @@
 
         @pl.when(m == g)
         def _():
+            @pl.when(owns)
+            def _():
+                for i in range(n_g):
+                    j = lax.rem(g + i, n_g)
+                    if i:
+                        y_arrived(second, j).wait_recv()
+                    for to in range(n_r):
+
+                        @pl.when(to != p)
+                        def _():
+                            y_pass(second, j, to).start()
+
             for j in range(n_g):
                 for s in range(2):
 
-                    @pl.when(jnp.logical_or(j != g, p != first + s))
+                    @pl.when(p != first + s)
                     def _():
                         y_arrived(s, j).wait_recv()
 
@@ -381,13 +404,16 @@
         def _():
             lax.fori_loop(1, n_d, split, 0)
 
-        @pl.when(m == g + 1)
-        def _():
-            lax.fori_loop(n_d, n_a, push, 0)
-
-        return carry
-
-    relay()
+        @pl.when(m > g)
+        def _():
+            left = n_a - n_d
+            steps = jnp.maximum(n_g - 1 - g, 1)
+            lax.fori_loop(
+                n_d + left * (m - g - 1) // steps, n_d + left * (m - g) // steps, push, 0
+            )
+
+        return carry
+
     lax.fori_loop(0, n_g, one_pair, 0)
 
     @pl.when(g == n_g - 1)
@@ -430,11 +456,19 @@
         @pl.when(jnp.logical_or(p == first, p == first + 1))
         def _():
             t_copy(d, first).wait_send()
-            for to in range(n_r):
-
-                @pl.when(jnp.logical_or(to != p, m != g))
-                def _():
-                    y_copy(d, second, m, to).wait_send()
+
+            @pl.when(m != g)
+            def _():
+                y_copy(d, second, m, p).wait_send()
+
+            @pl.when(m == g)
+            def _():
+                for j in range(n_g):
+                    for to in range(n_r):
+
+                        @pl.when(to != p)
+                        def _():
+                            y_pass(second, j, to).wait_send()
 
         return carry
 
@@ -513,11 +547,12 @@
             dma((n_d,)),
             dma((n_d, n_r)),
             dma((2, n_g)),
+            dma((n_g, n_r)),
             dma((n_a, n_g)),
             dma((n_a, n_g)),
         ],
         compiler_params=pltpu.CompilerParams(
-            collective_id=0, has_side_effects=True, vmem_limit_bytes=60 * 1024 * 1024
+            collective_id=0, has_side_effects=True, vmem_limit_bytes=48 * 1024 * 1024
         ),
         cost_estimate=pl.CostEstimate(
             flops=2 * n_a * sw * n_g * 2 * nb * nb,

time: 109 us -> 104 us (0.954)
  Pallas kernels: 99.7 us -> 96.3 us
    pallas_call x1, Pallas kernels: 99.7 us -> 96.3 us  [shards(): pl.pallas_call(functools.partial(kernel, n_r, n_g), out_shape=(jax.ShapeD...]
    unnamed x2 -> x4, local copies, waits for them, and re-layouts: 4.29 us -> 4.49 us
where the time goes in v4:
time: 104 us
  Pallas kernels  96.3 us (93%)
  local copies, waits for them, and re-layouts  5.69 us (5%)
  other arithmetic  1.68 us (2%)
    pallas_call x1, Pallas kernels, shards(): pl.pallas_call(functools.partial(kernel, n_r, n_g), out_shape=(jax.ShapeD...  96.3 us
    unnamed x4, local copies, waits for them, and re-layouts  4.49 us

profile of v4, /device:TPU:0, one launch (start us, length us, event | category | flops | bytes accessed | tf_op | source)
XLA Modules:
  0.0 104.3 jit_solution(14615609094671203093)
XLA Ops:
  0.6 1.7 %convert_element_type.3 = bf16[64,12,4,64]{3,2,1,0:T(4,128)(2,1)S(1)} convert(f32[64,12,4,64]{3,2,1,0:T(4,128)} %param.5) | non-fusion elementwise | flops 196608 | bytes 1179648 | tf_op jit(solution)/shard_map/convert_element_type | solution.py:506
  2.3 0.9 copy.9
  3.2 0.3 reshape.11.packed
  3.5 0.0 copy-start
  3.5 2.2 %copy-done = f32[1,2,1024,512]{3,2,1,0:T(8,128)S(1)} copy-done((f32[1,2,1024,512]{3,2,1,0:T(8,128)S(1)}, f32[1,2,1024,512]{3,2,1,0:T(8,128)}, u32[]{:S(2)}) %copy-start) | copy-done | bytes 4194328
  5.7 96.3 %shard_map.50 = (f32[2,32,512]{2,1,0:T(8,128)S(1)}, f32[10,32,512]{2,1,0:T(8,128)S(1)}) custom-call(bf16[12,512,512]{2,1,0:T(8,128)(2,1)} %bitcast.15, f32[2,1024,512]{2,1,0:T(8,128)S(1)} %bitcast.12, bf16[2,4,6,32,128]{4,3,2,1,0:T(8,128)(2,1)S(1)} %reshape.11.packed), custom_call_target="tpu_custom_call" | custom-call | flops 1610612736 | bytes 12582912 | tf_op jit(solution)/shard_map/pallas_call | solution.py:514
  102.0 0.8 copy.6
  102.8 1.5 %copy.7 = f32[32,10,1,512]{3,2,1,0:T(1,128)} copy(f32[32,10,1,512]{3,0,1,2:T(8,128)S(1)} %bitcast.13) | data formatting | bytes 1310720
Async XLA Ops:
  3.5 2.2 %copy-start = (f32[1,2,1024,512]{3,2,1,0:T(8,128)S(1)}, f32[1,2,1024,512]{3,2,1,0:T(8,128)}, u32[]{:S(2)}) copy-start(f32[1,2,1024,512]{3,2,1,0:T(8,128)} %param.4) | copy-start | bytes 12582916
